TPU v7x, 512 devices: a whole 4x8x8 slice. The times are simulated.
512 devices in a mesh: fsdp: 16 (over z, y_lo), ctx: 32 (over y_hi, x, core).
Axes of the slice: x: 4, y: 8 (y_hi: 4, y_lo: 2; y = y_hi * 2 + y_lo), z: 8, core: 2. Of those that a mesh axis runs over, the one named last changes fastest.
Arguments:
- hidden: bfloat16 [16, 4096, 8192], P('fsdp', 'ctx'), may hold values from -6 to 6
- values: bfloat16 [16, 4096, 4096], P('fsdp', 'ctx'), may hold values from -6 to 6
- targets: bfloat16 [16, 4096, 4096], P('fsdp', 'ctx'), may hold values from -6 to 6
- dt_raw: float32 [16, 32, 4096], P('fsdp', None, 'ctx'), as said below
- proj_weight: bfloat16 [8192, 128], P('fsdp'), may hold values from -0.0234375 to 0.0234375
- a_log: float32 [32], replicated
- skip: float32 [32], replicated, may hold values from 0.5 to 1.5
Outputs:
- grad_w: float32 [8192, 128], P('fsdp')
- grad_a_log: float32 [32], replicated
- grad_skip: float32 [32], replicated
- loss: float32 [], replicated
Inputs may be any that keep to these rules, and one draw needn't show every extreme that they name: softplus(dt_raw) is the step size of a head at a position.
All inputs are finite; a program needn't handle non-finite values.
Results may differ from a plain program's by a relative error of at most 0.004.
Values may be sent and summed in bfloat16 or wider, within the bound.
A program may use at most 192 MiB of HBM per device.

v0:
```python
import math
import jax
import jax.numpy as jnp
from jax import lax
from jax.sharding import PartitionSpec as P

highest = lax.Precision.HIGHEST


def prefix(value, axis, join, neutral, backward):
    count, mine = (lax.axis_size(axis), lax.axis_index(axis))
    pieces = jax.tree.map(lambda part: lax.all_gather(part, axis), value)
    if backward:
        pieces = jax.tree.map(lambda part: part[::-1], pieces)
        mine = count - 1 - mine
    subtotal = jax.tree.map(
        lambda part, zero: jnp.full_like(part, 0) + jnp.asarray(zero, part.dtype), value, neutral
    )

    def hop(position, subtotal):
        longer = join(subtotal, jax.tree.map(lambda part: part[position], pieces))
        return jax.tree.map(lambda new, old: jnp.where(position < mine, new, old), longer, subtotal)

    return lax.fori_loop(0, count - 1, hop, subtotal)


def product(form, left, right):
    return jnp.einsum(form, left, right, preferred_element_type=jnp.float32)


def block_local(proj, step_size, decay_rate, vals, lower_mask):
    row_count = proj.shape[0]
    head_count = step_size.shape[0]
    state_width = proj.shape[1] // 2
    input_map = proj[:, :state_width]
    output_map = proj[:, state_width:]
    decay_sum = jnp.cumsum(step_size * decay_rate[:, None], axis=1)
    final = decay_sum[:, -1:]
    scores = jnp.dot(output_map, input_map.T, preferred_element_type=jnp.float32)
    within = jnp.where(
        lower_mask[None] > 0,
        jnp.exp(jnp.minimum(decay_sum[:, :, None] - decay_sum[:, None, :], 0.0)),
        0.0,
    )
    mixing = within * scores[None] * step_size[:, None, :]
    inputs = vals.reshape(row_count, head_count, vals.shape[1] // head_count)
    inner_out = product("hts,shp->thp", mixing.astype(jnp.bfloat16), inputs)
    to_end = jnp.exp(final - decay_sum)
    weight_end = to_end * step_size
    coef = (weight_end[:, None, :] * input_map.T.astype(jnp.float32)[None]).astype(jnp.bfloat16)
    local_state = product("hns,shp->hnp", coef, inputs)
    growth = jnp.exp(decay_sum)
    carry = jnp.exp(final[:, 0])
    return (
        input_map,
        output_map,
        step_size,
        decay_sum,
        within,
        mixing,
        inputs,
        to_end,
        weight_end,
        growth,
        local_state,
        carry,
        inner_out,
    )


def block_output(pack, state_in, wanted, skip_gain):
    (
        input_map,
        output_map,
        step_size,
        decay_sum,
        within,
        mixing,
        inputs,
        to_end,
        weight_end,
        growth,
        local_state,
        carry,
        inner_out,
    ) = pack
    state_bf = state_in.astype(jnp.bfloat16)
    from_state = product("hnp,tn->thp", state_bf, output_map)
    outputs = (
        inner_out
        + growth.T[:, :, None] * from_state
        + skip_gain[None, :, None] * inputs.astype(jnp.float32)
    )
    misfit = outputs - wanted.reshape(inputs.shape).astype(jnp.float32)
    return (misfit, from_state, state_bf)


def block_return(pack, from_state, state_bf, misfit, loss_scale):
    (
        input_map,
        output_map,
        step_size,
        decay_sum,
        within,
        mixing,
        inputs,
        to_end,
        weight_end,
        growth,
        local_state,
        carry,
        inner_out,
    ) = pack
    grad_out = misfit * loss_scale
    skip_part = jnp.sum(grad_out * inputs.astype(jnp.float32), axis=(0, 2))
    grad_bf = grad_out.astype(jnp.bfloat16)
    mix_grad = product("thp,shp->hts", grad_bf, inputs)
    score_grad = jnp.sum(within * mix_grad * step_size[:, None, :], axis=0)
    weighted = mix_grad * mixing
    sum_grad = (
        jnp.sum(weighted, axis=2)
        - jnp.sum(weighted, axis=1)
        + growth * jnp.sum(grad_out * from_state, axis=2).T
    )
    grown_bf = (growth.T[:, :, None] * grad_out).astype(jnp.bfloat16)
    entry_grad = product("thp,tn->hnp", grown_bf, output_map)
    score_bf = score_grad.astype(jnp.bfloat16)
    out_grad = product("thp,hnp->tn", grown_bf, state_bf) + product(
        "ts,sn->tn", score_bf, input_map
    )
    in_grad = product("ts,tn->sn", score_bf, output_map)
    return (entry_grad, (out_grad, in_grad, sum_grad, skip_part))


def block_finish(pack, partial_value, exit_grad, state_in, decay_rate):
    (
        input_map,
        output_map,
        step_size,
        decay_sum,
        within,
        mixing,
        inputs,
        to_end,
        weight_end,
        growth,
        local_state,
        carry,
        inner_out,
    ) = pack
    out_grad, in_grad, sum_grad, skip_part = partial_value
    exit_bf = exit_grad.astype(jnp.bfloat16)
    coef_grad = product("hnp,shp->hns", exit_bf, inputs)
    in_grad = in_grad + jnp.einsum("hns,hs->sn", coef_grad, weight_end, precision=highest)
    pulled = jnp.einsum("hns,sn->hs", coef_grad, input_map.astype(jnp.float32), precision=highest)
    end_weight = pulled * weight_end
    final_grad = jnp.sum(end_weight, axis=1) + carry * jnp.sum(exit_grad * state_in, axis=(1, 2))
    row_count = step_size.shape[1]
    last_mark = (jnp.arange(row_count) == row_count - 1).astype(jnp.float32)
    sum_grad = sum_grad - end_weight + final_grad[:, None] * last_mark[None, :]
    step_grad = jnp.cumsum(sum_grad[:, ::-1], axis=1)[:, ::-1]
    alog_part = decay_rate * jnp.sum(step_grad * step_size, axis=1)
    proj_grad = jnp.concatenate([in_grad, out_grad], axis=1).astype(jnp.bfloat16)
    return (proj_grad, alog_part, skip_part)


def chain_link(earlier, later):
    return (earlier[0] * later[0], later[1] + later[0][:, None, None] * earlier[1])


def local(hidden, values, targets, dt_raw, proj_weight, a_log, skip):
    row_count = hidden.shape[1]
    features = hidden[0]
    position = jnp.arange(row_count)
    lower_mask = (position[:, None] >= position[None, :]).astype(jnp.float32)
    picked = features
    projection = jnp.dot(
        picked,
        lax.all_gather(proj_weight, "fsdp", axis=0, tiled=True),
        preferred_element_type=jnp.float32,
    )
    proj_bf = projection.astype(jnp.bfloat16)
    step_size = jax.nn.softplus(dt_raw[0])
    decay_rate = -jnp.exp(a_log)
    sequences = lax.axis_size("fsdp")
    length = row_count * lax.axis_size("ctx")
    loss_scale = 1.0 / (values.shape[2] * math.sqrt(sequences * length))
    local_pack = block_local(proj_bf, step_size, decay_rate, values[0], lower_mask)
    carry = local_pack[11]
    local_state = local_pack[10]
    identity = (jnp.ones_like(carry), jnp.zeros_like(local_state))
    entry = prefix((carry, local_state), "ctx", chain_link, identity, False)
    state_in = entry[1]
    misfit, from_state, state_bf = block_output(local_pack, state_in, targets[0], skip)
    loss_part = 0.5 * loss_scale * jnp.sum(misfit * misfit)
    entry_grad, partial_value = block_return(local_pack, from_state, state_bf, misfit, loss_scale)
    later = prefix((carry, entry_grad), "ctx", chain_link, identity, True)
    proj_grad, alog_part, skip_part = block_finish(
        local_pack, partial_value, later[1], state_in, decay_rate
    )
    picked = features
    shard_grad = lax.psum_scatter(
        lax.dot_general(
            picked, proj_grad, (((0,), (0,)), ((), ())), preferred_element_type=jnp.float32
        ),
        "fsdp",
        scatter_dimension=0,
        tiled=True,
    )
    grad_w = lax.psum(shard_grad, "ctx")
    totals = lax.psum((loss_part, alog_part, skip_part), ("fsdp", "ctx"))
    return (grad_w, totals[1], totals[2], totals[0])


def solution(mesh):
    in_specs = (
        P("fsdp", "ctx", None),
        P("fsdp", "ctx", None),
        P("fsdp", "ctx", None),
        P("fsdp", None, "ctx"),
        P("fsdp", None),
        P(),
        P(),
    )
    out_specs = (P("fsdp", None), P(), P(), P())
    return jax.shard_map(local, mesh=mesh, in_specs=in_specs, out_specs=out_specs, check_vma=False)
```

profile of v0, /device:TPU:1, one launch (start us, length us, event | category | flops | bytes accessed | tf_op | source)
XLA Modules:
  0.0 1085.1 jit_solution(3268131084844295965)
XLA Ops:
  10.3 75.1 %all-gather.7.cloned.1.call-done = bf16[8192,128]{1,0:T(8,128)(2,1)} async-done(((bf16[512,128]{1,0:T(8,128)(2,1)}), bf16[8192,128]{1,0:T(8,128)(2,1)}) %all-gather.7.cloned.1.call-update) | async-done | bytes 2097168 | tf_op jit(solution)/shard_map/all_gather | solution.py:179
  85.4 2.5 fusion.12
  87.9 1.8 fusion.27
  92.0 84.0 %all-reduce = f32[1024]{0:T(1024)S(1)} all-reduce(f32[1024]{0:T(1024)S(1)} %dynamic-update-slice), channel_id=3, replica_groups=mesh['fsdp'=16,'ctx'=32] {'ctx'}, use_global_device_ids=true, to_apply=%add | all-reduce | flops 1024 | bytes 8192
  176.0 2.6 copy.33
  178.8 130.9 %all-gather.9.cloned.1.call-done = f32[1024,64,128]{2,1,0:T(8,128)} async-done(((f32[32,64,128]{2,1,0:T(8,128)}), f32[1024,64,128]{2,1,0:T(8,128)}) %all-gather.9.cloned.1.call-update) | async-done | bytes 33554448 | tf_op jit(solution)/shard_map/all_gather | solution.py:12
  309.7 46.7 %while.28 = (s32[]{:T(128)}, f32[32,64,128]{2,1,0:T(8,128)S(1)}, s32[]{:T(128)}, f32[32,32,64,128]{3,2,1,0:T(8,128)}, f32[32,32]{1,0:T(8,128)S(1)}, /*index=5*/s32[]{:T(128)}, s32[]{:T(128)}) while((s32[]{:T(128)}, f32[32,64,128]{2,1,0:T(8,128)S(1)}, s32[]{:T(128)}, f32[32,32,64,128]{3,2,1,0:T(8,128)}, f32[32,32]{1,0:T(8,128)S(1)}, ...), condition=%wide.region_2.3_spmd.clone, body=%wide.region_1.2_spmd.clone.sunk | while | flops 1048580 | bytes 3146225 | solution.py:24
  358.3 2.4 multiply_reduce_fusion
  363.6 3.7 fusion.10
  367.8 204.4 %all-gather.11.cloned.1.call-done = f32[1024,64,128]{2,1,0:T(8,128)} async-done(((f32[32,64,128]{2,1,0:T(8,128)}), f32[1024,64,128]{2,1,0:T(8,128)}) %all-gather.11.cloned.1.call-update) | async-done | bytes 33554448 | tf_op jit(solution)/shard_map/all_gather | solution.py:12
  572.1 23.3 %rev.12 = f32[32,32,64,128]{3,2,1,0:T(8,128)} reverse(f32[32,32,64,128]{3,2,1,0:T(8,128)} %bitcast.108), dimensions={0} | reverse | bytes 67108864 | tf_op jit(solution)/shard_map/rev | solution.py:14
  595.4 85.1 %while.29 = (s32[]{:T(128)}, f32[32,64,128]{2,1,0:T(8,128)}, s32[]{:T(128)}, f32[32,32,64,128]{3,2,1,0:T(8,128)}, f32[32,32]{1,0:T(8,128)S(1)}, /*index=5*/s32[]{:T(128)}, s32[]{:T(128)}) while((s32[]{:T(128)}, f32[32,64,128]{2,1,0:T(8,128)}, s32[]{:T(128)}, f32[32,32,64,128]{3,2,1,0:T(8,128)}, f32[32,32]{1,0:T(8,128)S(1)}, ...), condition=%wide.region_5.6_spmd.clone, body=%wide.region_4.5_spmd.clone.sunk | while | flops 1048580 | bytes 3146225 | solution.py:24
  595.4 2.4 fusion.74
  597.9 2.7 fusion.74
  600.6 2.7 fusion.74
  603.4 2.7 fusion.74
  606.1 2.7 fusion.74
  608.9 2.7 fusion.74
  611.6 2.7 fusion.74
  614.4 2.7 fusion.74
  617.1 2.7 fusion.74
  619.9 2.7 fusion.74
  622.7 2.7 fusion.74
  625.4 2.7 fusion.74
  628.2 2.7 fusion.74
  630.9 2.7 fusion.74
  633.7 2.7 fusion.74
  636.4 2.7 fusion.74
  639.2 2.7 fusion.74
  642.0 2.7 fusion.74
  644.7 2.7 fusion.74
  647.5 2.7 fusion.74
  650.2 2.7 fusion.74
  653.0 2.7 fusion.74
  655.7 2.7 fusion.74
  658.5 2.7 fusion.74
  661.2 2.7 fusion.74
  664.0 2.7 fusion.74
  666.8 2.7 fusion.74
  669.5 2.7 fusion.74
  672.3 2.7 fusion.74
  675.0 2.7 fusion.74
  677.8 2.7 fusion.74
  680.5 2.9 multiply_reduce_fusion.4
  683.6 2.6 convolution_bitcast_fusion
  690.8 97.0 %reduce-scatter.2.cloned.1.call-done = f32[512,128]{0,1:T(8,128)} async-done(((f32[8192,128]{0,1:T(8,128)}), f32[512,128]{0,1:T(8,128)}) %reduce-scatter.2.cloned.1.call-update) | async-done | bytes 262160 | tf_op jit(solution)/shard_map/reduce_scatter | solution.py:202
  788.0 98.9 %all-reduce.1 = (f32[32]{0:T(128)}, f32[32]{0:T(128)}, f32[]{:T(128)}) all-reduce(f32[32]{0:T(128)S(1)} %fusion.63, f32[32]{0:T(128)S(1)} %get-tuple-element.247, f32[]{:T(128)S(6)} %mul_shard_map.3), channel_id=1, replica_groups=mesh['fsdp'=16,'ctx'=32] {'fsdp','ctx'}, use_global_device_ids=true, to_apply=%region_15.16 | all-reduce | flops 65 | bytes 520 | tf_op jit(solution)/shard_map/psum | solution.py:211
  886.9 189.9 %all-reduce.4.cloned.1.call-done = f32[512,128]{0,1:T(8,128)} async-done(((f32[512,128]{0,1:T(8,128)}), f32[512,128]{0,1:T(8,128)}) %all-reduce.4.cloned.1.call-update) | async-done | bytes 262160 | tf_op jit(solution)/shard_map/psum | solution.py:210
  (157 shorter events, 62.0 us)
Async XLA Ops:
  7.2 78.2 %copy-start = (bf16[1,128,8192]{2,1,0:T(8,128)(2,1)S(1)}, bf16[1,128,8192]{2,1,0:T(8,128)(2,1)}, u32[]{:S(2)}) copy-start(bf16[1,128,8192]{2,1,0:T(8,128)(2,1)} %param.11) | copy-start | bytes 6291460
  7.2 2.4 copy-start.8
  7.2 2.5 copy-start.6
  7.2 78.2 %all-gather.7.cloned.1.call-start = ((), (), s32[]{:S(2)}) async-start(), calls=%async_computation.1 | async-start | bytes 2228224 | tf_op jit(solution)/shard_map/all_gather | solution.py:179
  7.9 301.7 %all-gather.9.cloned.1.call-start = ((), (), s32[]{:S(2)}) async-start(), calls=%async_computation.4 | async-start | bytes 34603008 | tf_op jit(solution)/shard_map/all_gather | solution.py:12
  9.6 78.3 %copy-start.1 = (bf16[1,128,4096]{1,2,0:T(8,128)(2,1)}, bf16[1,128,4096]{1,2,0:T(8,128)(2,1)S(1)}, u32[]{:S(2)}) copy-start(bf16[1,128,4096]{1,2,0:T(8,128)(2,1)S(1)} %copy.31) | copy-start | bytes 3145732
  89.7 482.4 %all-gather.11.cloned.1.call-start = ((), (), s32[]{:S(2)}) async-start(), calls=%async_computation.5 | async-start | bytes 34603008 | tf_op jit(solution)/shard_map/all_gather | solution.py:12
  356.4 1.2 copy-start.2
  356.4 1.9 copy-start.5
  356.4 1.9 copy-start.7
  360.7 1.4 copy-start.3
  363.5 424.3 %reduce-scatter.2.cloned.1.call-start = ((), (), s32[]{:S(2)}) async-start(), calls=%async_computation.2 | async-start | bytes 4456448 | tf_op jit(solution)/shard_map/reduce_scatter | solution.py:202
  363.6 3.8 copy-start.4
  686.2 390.5 %all-reduce.4.cloned.1.call-start = ((), (), s32[]{:S(2)}) async-start(), calls=%async_computation.3 | async-start | bytes 524288 | tf_op jit(solution)/shard_map/psum | solution.py:210
Sparse Core Ops, SparseCore 0:
  10.1 75.1 all-gather.6
  89.9 219.7 all-gather.8
  363.6 208.4 all-gather.10
  686.4 101.4 reduce-scatter.1
  790.6 286.1 all-reduce.3
where the time goes:
time: 1090 us
  waiting for transfers between devices  698 us (64%)
  blocking collectives  183 us (17%)
  other arithmetic  134 us (12%)
  local copies, waits for them, and re-layouts  34.6 us (3%)
  matrix products  18.7 us (2%)
  between operations  15.3 us (1%)
    all_gather x2, waiting for transfers between devices, prefix(): pieces = jax.tree.map(lambda part: lax.all_gather(part, axis), value)  335 us
    psum x1, waiting for transfers between devices, local(): grad_w = lax.psum(shard_grad, 'ctx')  190 us
    select_n x62, other arithmetic, hop(): jnp.where(position < mine, new, old)  130 us
    psum x1, blocking collectives, local(): totals = lax.psum((loss_part, alog_part, skip_part), ('fsdp', 'ctx'))  98.9 us
    reduce_scatter x1, waiting for transfers between devices, local(): lax.psum_scatter(lax.dot_general(picked, proj_grad, (((0,), (0,)), ((), (...  97 us
    unnamed x1, blocking collectives  84 us
    all_gather x1, waiting for transfers between devices, local(): lax.all_gather(proj_weight, 'fsdp', axis=0, tiled=True)  75.1 us
    rev x2, local copies, waits for them, and re-layouts, prefix(): pieces = jax.tree.map(lambda part: part[::-1], pieces)  23.3 us
  transfers between devices with their start and end apart: 5, of which 5 were waited for; matrix products, arithmetic and copies ran while one was open for 1% of the time, Pallas kernels for 0%

commit v1 on v0

--- a/solution.py
+++ b/solution.py
@@ -207,7 +207,7 @@
         scatter_dimension=0,
         tiled=True,
     )
-    grad_w = lax.psum(shard_grad, "ctx")
+    grad_w = jnp.sum(lax.all_gather(shard_grad, "ctx"), axis=0)
     totals = lax.psum((loss_part, alog_part, skip_part), ("fsdp", "ctx"))
     return (grad_w, totals[1], totals[2], totals[0])
 

time: 1090 us -> 921 us (0.84)
  waiting for transfers between devices: 698 us -> 513 us
    psum x1 -> x0, waiting for transfers between devices: 190 us -> none  [local(): grad_w = lax.psum(shard_grad, 'ctx')]
  transfers between devices with their start and end apart: 5 -> 5, of which waited for: 5 -> 4; matrix products, arithmetic and copies ran while one was open for 1% -> 2% of each run, Pallas kernels for 0% -> 0%
where the time goes in v1:
time: 921 us; the launch traced here: 918 us
  waiting for transfers between devices  513 us (56%)
  blocking collectives  189 us (21%)
  other arithmetic  137 us (15%)
  local copies, waits for them, and re-layouts  43.5 us (5%)
  matrix products  18.8 us (2%)
  between operations  15.3 us (2%)
    all_gather x2, waiting for transfers between devices, prefix(): pieces = jax.tree.map(lambda part: lax.all_gather(part, axis), value)  335 us
    select_n x62, other arithmetic, hop(): jnp.where(position < mine, new, old)  130 us
    psum x1, blocking collectives, local(): totals = lax.psum((loss_part, alog_part, skip_part), ('fsdp', 'ctx'))  105 us
    reduce_scatter x1, waiting for transfers between devices, local(): lax.psum_scatter(lax.dot_general(picked, proj_grad, (((0,), (0,)), ((), (...  102 us
    unnamed x1, blocking collectives  84 us
    all_gather x1, waiting for transfers between devices, local(): lax.all_gather(proj_weight, 'fsdp', axis=0, tiled=True)  75.1 us
    rev x2, local copies, waits for them, and re-layouts, prefix(): pieces = jax.tree.map(lambda part: part[::-1], pieces)  23.3 us
  transfers between devices with their start and end apart: 5, of which 4 were waited for; matrix products, arithmetic and copies ran while one was open for 2% of the time, Pallas kernels for 0%

profile of v1, /device:TPU:1, one launch (start us, length us, event | category | flops | bytes accessed | tf_op | source)
XLA Modules:
  0.0 917.5 jit_solution(11729016954966226366)
XLA Ops:
  10.3 75.1 %all-gather.9.cloned.1.call-done = bf16[8192,128]{1,0:T(8,128)(2,1)} async-done(((bf16[512,128]{1,0:T(8,128)(2,1)}), bf16[8192,128]{1,0:T(8,128)(2,1)}) %all-gather.9.cloned.1.call-update) | async-done | bytes 2097168 | tf_op jit(solution)/shard_map/all_gather | solution.py:179
  85.4 2.5 fusion.12
  92.0 84.0 %all-reduce = f32[1024]{0:T(1024)S(1)} all-reduce(f32[1024]{0:T(1024)S(1)} %dynamic-update-slice), channel_id=3, replica_groups=mesh['fsdp'=16,'ctx'=32] {'ctx'}, use_global_device_ids=true, to_apply=%add | all-reduce | flops 1024 | bytes 8192
  176.0 2.6 copy.31
  178.8 130.9 %all-gather.11.cloned.1.call-done = f32[1024,64,128]{2,1,0:T(8,128)} async-done(((f32[32,64,128]{2,1,0:T(8,128)}), f32[1024,64,128]{2,1,0:T(8,128)}) %all-gather.11.cloned.1.call-update) | async-done | bytes 33554448 | tf_op jit(solution)/shard_map/all_gather | solution.py:12
  309.7 46.7 %while.28 = (s32[]{:T(128)}, f32[32,64,128]{2,1,0:T(8,128)S(1)}, s32[]{:T(128)}, f32[32,32,64,128]{3,2,1,0:T(8,128)}, f32[32,32]{1,0:T(8,128)S(1)}, /*index=5*/s32[]{:T(128)}, s32[]{:T(128)}) while((s32[]{:T(128)}, f32[32,64,128]{2,1,0:T(8,128)S(1)}, s32[]{:T(128)}, f32[32,32,64,128]{3,2,1,0:T(8,128)}, f32[32,32]{1,0:T(8,128)S(1)}, ...), condition=%wide.region_2.3_spmd.clone, body=%wide.region_1.2_spmd.clone.sunk | while | flops 1048580 | bytes 3146225 | solution.py:24
  358.3 2.4 multiply_reduce_fusion
  363.6 3.7 fusion.10
  367.8 204.3 %all-gather.13.cloned.1.call-done = f32[1024,64,128]{2,1,0:T(8,128)} async-done(((f32[32,64,128]{2,1,0:T(8,128)}), f32[1024,64,128]{2,1,0:T(8,128)}) %all-gather.13.cloned.1.call-update) | async-done | bytes 33554448 | tf_op jit(solution)/shard_map/all_gather | solution.py:12
  572.1 23.3 %rev.12 = f32[32,32,64,128]{3,2,1,0:T(8,128)} reverse(f32[32,32,64,128]{3,2,1,0:T(8,128)} %bitcast.113), dimensions={0} | reverse | bytes 67108864 | tf_op jit(solution)/shard_map/rev | solution.py:14
  595.4 85.1 %while.29 = (s32[]{:T(128)}, f32[32,64,128]{2,1,0:T(8,128)}, s32[]{:T(128)}, f32[32,32,64,128]{3,2,1,0:T(8,128)}, f32[32,32]{1,0:T(8,128)S(1)}, /*index=5*/s32[]{:T(128)}, s32[]{:T(128)}) while((s32[]{:T(128)}, f32[32,64,128]{2,1,0:T(8,128)}, s32[]{:T(128)}, f32[32,32,64,128]{3,2,1,0:T(8,128)}, f32[32,32]{1,0:T(8,128)S(1)}, ...), condition=%wide.region_5.6_spmd.clone, body=%wide.region_4.5_spmd.clone.sunk | while | flops 1048580 | bytes 3146225 | solution.py:24
  595.4 2.4 fusion.74
  597.9 2.7 fusion.74
  600.6 2.7 fusion.74
  603.4 2.7 fusion.74
  606.1 2.7 fusion.74
  608.9 2.7 fusion.74
  611.6 2.7 fusion.74
  614.4 2.7 fusion.74
  617.1 2.7 fusion.74
  619.9 2.7 fusion.74
  622.7 2.7 fusion.74
  625.4 2.7 fusion.74
  628.2 2.7 fusion.74
  630.9 2.7 fusion.74
  633.7 2.7 fusion.74
  636.4 2.7 fusion.74
  639.2 2.7 fusion.74
  641.9 2.7 fusion.74
  644.7 2.7 fusion.74
  647.5 2.7 fusion.74
  650.2 2.7 fusion.74
  653.0 2.7 fusion.74
  655.7 2.7 fusion.74
  658.5 2.7 fusion.74
  661.2 2.7 fusion.74
  664.0 2.7 fusion.74
  666.8 2.7 fusion.74
  669.5 2.7 fusion.74
  672.3 2.7 fusion.74
  675.0 2.7 fusion.74
  677.8 2.7 fusion.74
  680.5 3.0 multiply_reduce_fusion.4
  683.7 2.6 convolution_bitcast_fusion
  686.4 101.5 %reduce-scatter.2.cloned.1.call-done = f32[512,128]{0,1:T(8,128)} async-done(((f32[8192,128]{0,1:T(8,128)}), f32[512,128]{0,1:T(8,128)}) %reduce-scatter.2.cloned.1.call-update) | async-done | bytes 262160 | tf_op jit(solution)/shard_map/reduce_scatter | solution.py:202
  792.7 104.9 %all-reduce.1 = (f32[32]{0:T(128)}, f32[32]{0:T(128)}, f32[]{:T(128)}) all-reduce(f32[32]{0:T(128)S(1)} %fusion.63, f32[32]{0:T(128)S(1)} %get-tuple-element.239, f32[]{:T(128)S(6)} %mul_shard_map.3), channel_id=1, replica_groups=mesh['fsdp'=16,'ctx'=32] {'fsdp','ctx'}, use_global_device_ids=true, to_apply=%region_15.16 | all-reduce | flops 65 | bytes 520 | tf_op jit(solution)/shard_map/psum | solution.py:211
  897.6 9.9 %copy.60 = f32[16,8,32,512]{3,2,1,0:T(8,128)S(1)} copy(f32[16,8,32,512]{3,1,2,0:T(8,128)} %bitcast.118) | data formatting | bytes 16777216
  907.5 2.7 bitcast_reduce_fusion
  (159 shorter events, 62.9 us)
Async XLA Ops:
  7.2 78.2 %copy-start = (bf16[1,128,8192]{2,1,0:T(8,128)(2,1)S(1)}, bf16[1,128,8192]{2,1,0:T(8,128)(2,1)}, u32[]{:S(2)}) copy-start(bf16[1,128,8192]{2,1,0:T(8,128)(2,1)} %param.11) | copy-start | bytes 6291460
  7.2 2.4 copy-start.8
  7.2 2.5 copy-start.6
  7.2 78.2 %all-gather.9.cloned.1.call-start = ((), (), s32[]{:S(2)}) async-start(), calls=%async_computation.1 | async-start | bytes 2228224 | tf_op jit(solution)/shard_map/all_gather | solution.py:179
  7.9 301.8 %all-gather.11.cloned.1.call-start = ((), (), s32[]{:S(2)}) async-start(), calls=%async_computation.3 | async-start | bytes 34603008 | tf_op jit(solution)/shard_map/all_gather | solution.py:12
  9.6 78.3 %copy-start.1 = (bf16[1,128,4096]{1,2,0:T(8,128)(2,1)}, bf16[1,128,4096]{1,2,0:T(8,128)(2,1)S(1)}, u32[]{:S(2)}) copy-start(bf16[1,128,4096]{1,2,0:T(8,128)(2,1)S(1)} %copy.29) | copy-start | bytes 3145732
  89.7 482.4 %all-gather.13.cloned.1.call-start = ((), (), s32[]{:S(2)}) async-start(), calls=%async_computation.4 | async-start | bytes 34603008 | tf_op jit(solution)/shard_map/all_gather | solution.py:12
  356.4 1.2 copy-start.2
  356.4 1.9 copy-start.5
  356.4 1.9 copy-start.7
  360.7 1.4 copy-start.3
  363.5 424.4 %reduce-scatter.2.cloned.1.call-start = ((), (), s32[]{:S(2)}) async-start(), calls=%async_computation.2 | async-start | bytes 4456448 | tf_op jit(solution)/shard_map/reduce_scatter | solution.py:202
  363.6 3.8 copy-start.4
  686.3 211.3 %all-gather.15.cloned.1.call-start = ((), (), s32[]{:S(2)}) async-start(), calls=%async_computation.5 | async-start | bytes 8650752 | tf_op jit(solution)/shard_map/all_gather | solution.py:210
Sparse Core Ops, SparseCore 0:
  10.1 75.1 all-gather.8
  89.9 219.8 all-gather.10
  363.7 208.4 all-gather.12
  686.5 101.4 reduce-scatter.1
  790.9 80.1 all-gather.14
